TPU v7x, 32 devices: a whole 2x2x4 slice. The times are simulated.
32 devices in a mesh: node: 8 (over z, y), local: 4 (over x, core).
Axes of the slice: x: 2, y: 2, z: 4, core: 2. Of those that a mesh axis runs over, the one named last changes fastest.
Arguments:
- tokens: bfloat16 [4096, 2048], P(('node', 'local')), may hold values from -6 to 6
- group_choice: int32 [4096, 4], P(('node', 'local')), may hold values from 0 to 7, as said below
- members: int32 [4096, 8], P(('node', 'local')), may hold values from 0 to 3, as said below
- route_weight: float32 [4096, 8], P(('node', 'local')), may hold values from 0.1 to 1
- expert_home: int32 [32], replicated, may hold values from 0 to 31, as said below
- expert_gate: bfloat16 [32, 2048, 768], P(('node', 'local')), may hold values from -0.125 to 0.125
- expert_up: bfloat16 [32, 2048, 768], P(('node', 'local')), may hold values from -0.125 to 0.125
- expert_down: bfloat16 [32, 768, 2048], P(('node', 'local')), may hold values from -0.21875 to 0.21875
- shared_gate: bfloat16 [2048, 1024], P(None, 'local'), may hold values from -0.125 to 0.125
- shared_up: bfloat16 [2048, 1024], P(None, 'local'), may hold values from -0.125 to 0.125
- shared_down: bfloat16 [1024, 2048], P('local'), may hold values from -0.1875 to 0.1875
Outputs:
- layer_out: bfloat16 [4096, 2048], P(('node', 'local'))
Inputs may be any that keep to these rules, and one draw needn't show every extreme that they name: `group_choice`: each row names 4 different groups. `members`: entries 2j and 2j + 1 of a row differ. `expert_home`: A permutation; the experts of each group (consecutive blocks of 4) lie on the devices with indices in that same block.
All inputs are finite; a program needn't handle non-finite values.
Results may differ from a plain program's by a relative error of at most 0.0056.
Values may be sent and summed in bfloat16 or wider, within the bound.
No kernel may reach another device: no remote copies, remote signals or barrier semaphores. Data moves between devices by JAX's collectives and lax.ppermute only.
A program may use at most 128 MiB of HBM per device.

v0:
```python
import jax
import jax.numpy as jnp
from jax import lax
from jax.sharding import PartitionSpec as P

GROUPS = 8


def per_device(
    tokens,
    group_choice,
    members,
    route_weight,
    expert_home,
    expert_gate,
    expert_up,
    expert_down,
    shared_gate,
    shared_up,
    shared_down,
):
    node_count = lax.axis_size("node")
    local_count = lax.axis_size("local")
    device_count = node_count * local_count
    tok_rows, model_width = tokens.shape
    top_count = members.shape[1]
    experts_all = expert_home.shape[0]
    per_group = experts_all // GROUPS
    capacity = 2 * tok_rows * top_count // experts_all
    chosen = jnp.repeat(group_choice, 2, axis=1) * per_group + members
    onehot = (chosen[:, :, None] == jnp.arange(experts_all, dtype=jnp.int32)[None, None, :]).astype(
        jnp.int32
    )
    target = jnp.sum(onehot * expert_home[None, None, :], axis=-1)
    flat_hits = onehot.reshape(tok_rows * top_count, experts_all)
    before = jnp.cumsum(flat_hits, axis=0) - flat_hits
    position = jnp.sum(before * flat_hits, axis=-1).reshape(tok_rows, top_count)
    keep_mask = position < capacity
    slot_index = jnp.where(keep_mask, target * capacity + position, device_count * capacity)
    token_id = jnp.broadcast_to(
        jnp.arange(tok_rows, dtype=jnp.int32)[:, None], (tok_rows, top_count)
    )
    source_row = (
        jnp.full((device_count * capacity,), tok_rows, jnp.int32)
        .at[slot_index.reshape(-1)]
        .set(token_id.reshape(-1), mode="drop")
    )
    padded = jnp.concatenate([tokens, jnp.zeros((1, model_width), tokens.dtype)], axis=0)
    outgoing = padded[source_row].reshape(device_count, capacity, model_width)
    local_gate = expert_gate[0]
    local_up = expert_up[0]
    local_down = expert_down[0]
    arrived = lax.all_to_all(outgoing, ("node", "local"), split_axis=0, concat_axis=0, tiled=True)
    block_shape = arrived.shape
    row_block = arrived.reshape(-1, model_width)
    gate_part = jnp.dot(row_block, local_gate, preferred_element_type=jnp.float32)
    up_part = jnp.dot(row_block, local_up, preferred_element_type=jnp.float32)
    hidden = (jax.nn.silu(gate_part) * up_part).astype(jnp.bfloat16)
    result = jnp.dot(hidden, local_down, preferred_element_type=jnp.float32).astype(jnp.bfloat16)
    answered = lax.all_to_all(
        result.reshape(block_shape), ("node", "local"), split_axis=0, concat_axis=0, tiled=True
    )
    answered = answered.reshape(device_count * capacity, model_width)
    picked = answered[jnp.minimum(slot_index, device_count * capacity - 1)]
    weight = jnp.where(keep_mask, route_weight, 0.0)
    routed = jnp.zeros((tok_rows, model_width), jnp.float32)
    for choice_index in range(top_count):
        routed = routed + weight[:, choice_index, None] * picked[:, choice_index].astype(
            jnp.float32
        )
    node_rows = lax.all_gather(tokens, "local", axis=0, tiled=True)
    shared_hidden = (
        jax.nn.silu(jnp.dot(node_rows, shared_gate, preferred_element_type=jnp.float32))
        * jnp.dot(node_rows, shared_up, preferred_element_type=jnp.float32)
    ).astype(jnp.bfloat16)
    shared_part = lax.psum_scatter(
        jnp.dot(shared_hidden, shared_down, preferred_element_type=jnp.float32),
        "local",
        scatter_dimension=0,
        tiled=True,
    )
    return (routed + shared_part).astype(jnp.bfloat16)


def solution(mesh):
    in_specs = (
        P(("node", "local"), None),
        P(("node", "local"), None),
        P(("node", "local"), None),
        P(("node", "local"), None),
        P(),
        P(("node", "local"), None, None),
        P(("node", "local"), None, None),
        P(("node", "local"), None, None),
        P(None, "local"),
        P(None, "local"),
        P("local", None),
    )
    out_specs = P(("node", "local"), None)
    return jax.shard_map(
        per_device, mesh=mesh, in_specs=in_specs, out_specs=out_specs, check_vma=False
    )
```

profile of v0, /device:TPU:0, one launch (start us, length us, event | category | flops | bytes accessed | tf_op | source)
XLA Modules:
  0.0 512.1 jit_solution(6456572306052749587)
XLA Ops:
  6.5 0.8 broadcast_multiply_fusion.1
  7.4 0.8 add.87
  8.5 9.0 %reduce-window.6 = s32[32,8,128]{2,1,0:T(8,128)S(1)} reduce-window(s32[32,8,128]{2,1,0:T(8,128)S(1)} %fusion.26, s32[]{:T(128)} %constant.11.clone.1), window={size=1x1x128 pad=0_0x0_0x127_0}, to_apply=%region_0.0 | reduce-window | flops 4161536 | bytes 262148 | tf_op jit(solution)/shard_map/reduce-window
  17.6 0.1 copy.43
  18.0 0.7 select_reduce_fusion
  19.1 4.3 scatter_custom_fusion
  23.4 2.0 concatenate.3
  25.4 17.5 %gather_fusion = bf16[2048,2048]{1,0:T(8,128)(2,1)} fusion(bf16[129,2048]{1,0:T(8,128)(2,1)} %concatenate.3, s32[2048]{0:T(1024)S(1)} %fusion.27), kind=kCustom, calls=%fused_computation | custom fusion | bytes 16785408 | tf_op jit(solution)/shard_map/gather | solution.py:49
  42.9 190.8 %all_to_all.10 = bf16[32,64,2048]{2,1,0:T(8,128)(2,1)S(1)} all-to-all(bf16[32,64,2048]{2,1,0:T(8,128)(2,1)} %bitcast.94), channel_id=1, replica_groups=mesh['node'=8,'local'=4] {'node','local'}, dimensions={0} | all-to-all | bytes 16777216 | tf_op jit(solution)/shard_map/all_to_all | solution.py:53
  233.7 3.2 copy-done.2
  236.9 8.5 %fusion.3 = f32[2048,768]{1,0:T(8,128)} fusion(bf16[2048,2048]{1,0:T(8,128)(2,1)S(1)} %bitcast.96, bf16[1,2048,768]{2,1,0:T(8,128)(2,1)S(1)} %copy-done.6), kind=kOutput, calls=%fused_computation.7 | convolution fusion | flops 6442450944 | bytes 17825792 | tf_op jit(solution)/shard_map/dot_general | solution.py:56
  245.4 21.3 %convolution_convert_fusion = bf16[2048,2048]{1,0:T(8,128)(2,1)} fusion(f32[2048,768]{1,0:T(8,128)} %fusion.3, bf16[2048,2048]{1,0:T(8,128)(2,1)} %bitcast.97, bf16[1,768,2048]{2,1,0:T(8,128)(2,1)S(1)} %copy-done, bf16[1,2048,768]{2,1,0:T(8,128)(2,1)} %param.17), kind=kOutput, calls=%fused_computation.3 | convolution fusion | flops 12898533376 | bytes 29360128 | tf_op jit(solution)/shard_map/dot_general | solution.py:59
  266.7 4.0 all-to-all-start.1
  270.8 0.7 all-gather.2.cloned.1.call-update
  271.5 0.2 reduce-scatter.2.cloned.1.call-start
  271.7 69.0 %all-gather.2.cloned.1.call-done = bf16[512,2048]{1,0:T(8,128)(2,1)} async-done(((bf16[128,2048]{1,0:T(8,128)(2,1)}), bf16[512,2048]{1,0:T(8,128)(2,1)}) %all-gather.2.cloned.1.call-update) | async-done | bytes 2097168 | tf_op jit(solution)/shard_map/all_gather | solution.py:71
  340.7 3.5 fusion.35
  344.2 5.6 %fusion.7 = f32[512,2048]{1,0:T(8,128)} fusion(bf16[256,2048]{1,0:T(8,128)(2,1)S(1)} %copy-done.4, bf16[512,2048]{1,0:T(8,128)(2,1)S(1)} %copy-done.3, bf16[2048,256]{1,0:T(8,128)(2,1)} %param.20, f32[512,256]{1,0:T(8,128)} %fusion.35), kind=kOutput, calls=%fused_computation.12 | convolution fusion | flops 1074528256 | bytes 8912896 | tf_op jit(solution)/shard_map/dot_general | solution.py:77
  350.3 0.2 copy-done.5
  350.6 0.4 slice_reduce_fusion.7
  351.0 108.2 %all-to-all-done.1 = bf16[32,64,2048]{2,1,0:T(8,128)(2,1)} async-done(((bf16[32,64,2048]{2,1,0:T(8,128)(2,1)}), bf16[32,64,2048]{2,1,0:T(8,128)(2,1)}, u32[]{:S(2)}, u32[]{:S(2)}) %all-to-all-start.1) | async-done | bytes 8388640 | tf_op jit(solution)/shard_map/all_to_all | solution.py:60
  459.2 13.3 %gather_fusion.1 = bf16[1024,2048]{1,0:T(8,128)(2,1)} fusion(bf16[2048,2048]{1,0:T(8,128)(2,1)} %bitcast.11, s32[1024]{0:T(1024)S(1)} %broadcast_clamp_fusion), kind=kCustom, calls=%fused_computation.1 | custom fusion | bytes 8392704 | tf_op jit(solution)/shard_map/gather | solution.py:64
  472.5 23.4 %fusion.34 = (bf16[128,1,2048]{2,1,0:T(2,128)(2,1)}, bf16[128,1,2048]{2,1,0:T(2,128)(2,1)}, bf16[128,1,2048]{2,1,0:T(2,128)(2,1)}, bf16[128,1,2048]{2,1,0:T(2,12...) fusion(bf16[128,8,2048]{2,1,0:T(8,128)(2,1)} %bitcast.93), kind=kLoop, calls=%fused_computation.79 | loop fusion | bytes 8388608 | tf_op jit(solution)/shard_map/slice | solution.py:68
  495.9 9.3 %fusion.10 = bf16[128,2048]{1,0:T(8,128)(2,1)} fusion(f32[128,2048]{1,0:T(8,128)} %reduce-scatter.2.cloned.1.call-done, bf16[128,1,2048]{2,1,0:T(2,128)(2,1)} %get-tuple-element.20, bf16[128,1,2048]{2,1,0:T(2,128)(2,1)} %get-tuple-element.14, bf16[128,1,2048]{2,1,0:T(2,128)(2,1)} %get-tuple-element.15, bf16[128,1,2048]{2,1,0:T(2,128)(2,1)} %get-tuple-element.16, ...), kind=kLoop, calls=%fused_computation.16 | loop fusion | flops 6553600 | bytes 5771264 | tf_op jit(solution)/shard_map/convert_element_type | solution.py:82
  (43 shorter events, 1.6 us)
Async XLA Ops:
  6.5 238.9 %copy-start = (bf16[1,768,2048]{2,1,0:T(8,128)(2,1)S(1)}, bf16[1,768,2048]{2,1,0:T(8,128)(2,1)}, u32[]{:S(2)}) copy-start(bf16[1,768,2048]{2,1,0:T(8,128)(2,1)} %param.18) | copy-start | bytes 9437188
  42.9 194.1 %copy-start.6 = (bf16[1,2048,768]{2,1,0:T(8,128)(2,1)S(1)}, bf16[1,2048,768]{2,1,0:T(8,128)(2,1)}, u32[]{:S(2)}) copy-start(bf16[1,2048,768]{2,1,0:T(8,128)(2,1)} %param.16) | copy-start | bytes 9437188
  233.7 3.2 copy-start.2
  266.7 192.5 %all-to-all-start.1 = ((bf16[32,64,2048]{2,1,0:T(8,128)(2,1)}), bf16[32,64,2048]{2,1,0:T(8,128)(2,1)}, u32[]{:S(2)}, u32[]{:S(2)}) async-start(bf16[32,64,2048]{2,1,0:T(8,128)(2,1)} %bitcast.95), calls=%async_computation.1 | async-start | bytes 16777216 | tf_op jit(solution)/shard_map/all_to_all | solution.py:60
  270.7 73.5 %copy-start.4 = (bf16[256,2048]{1,0:T(8,128)(2,1)S(1)}, bf16[256,2048]{1,0:T(8,128)(2,1)}, u32[]{:S(2)}) copy-start(bf16[256,2048]{1,0:T(8,128)(2,1)} %param.21) | copy-start | bytes 3145732
  270.7 70.0 %all-gather.2.cloned.1.call-start = ((), (), s32[]{:S(2)}) async-start(), calls=%async_computation.3 | async-start | bytes 2621440 | tf_op jit(solution)/shard_map/all_gather | solution.py:71
  271.5 224.4 %reduce-scatter.2.cloned.1.call-start = ((), (), s32[]{:S(2)}) async-start(), calls=%async_computation.4 | async-start | bytes 5242880 | tf_op jit(solution)/shard_map/reduce_scatter | solution.py:76
  340.7 3.5 copy-start.3
  349.8 0.7 copy-start.5
  495.9 9.3 %copy-start.1 = (bf16[1,768,2048]{2,1,0:T(8,128)(2,1)S(1)}, bf16[1,768,2048]{2,1,0:T(8,128)(2,1)}, u32[]{:S(2)}) copy-start(bf16[1,768,2048]{2,1,0:T(8,128)(2,1)} %param.18) | copy-start | bytes 9437188
Sparse Core Ops, SparseCore 0:
  273.1 67.5 all-gather.1
  349.9 51.1 reduce-scatter.1
where the time goes:
time: 512 us
  blocking collectives  191 us (37%)
  waiting for transfers between devices  178 us (35%)
  local copies, waits for them, and re-layouts  65.6 us (13%)
  matrix products  38.9 us (8%)
  other arithmetic  21 us (4%)
  between operations  13.6 us (3%)
    all_to_all x1, blocking collectives, per_device(): lax.all_to_all(outgoing, ('node', 'local'), split_axis=0, concat_axis=0,...  191 us
    all_to_all x1, waiting for transfers between devices, per_device(): lax.all_to_all(result.reshape(block_shape), ('node', 'local'), split_axis...  108 us
    all_gather x1, waiting for transfers between devices, per_device(): node_rows = lax.all_gather(tokens, 'local', axis=0, tiled=True)  69 us
    slice x1, local copies, waits for them, and re-layouts, per_device(): picked[:, choice_index].astype(jnp.float32)  23.4 us
    dot_general x1, matrix products, per_device(): jnp.dot(hidden, local_down, preferred_element_type=jnp.float32)  21.3 us
    gather x1, local copies, waits for them, and re-layouts, per_device(): outgoing = padded[source_row].reshape(device_count, capacity, model_width)  17.5 us
    gather x1, local copies, waits for them, and re-layouts, per_device(): picked = answered[jnp.minimum(slot_index, device_count * capacity - 1)]  13.3 us
  transfers between devices with their start and end apart: 3, of which 2 were waited for; matrix products, arithmetic and copies ran while one was open for 9% of the time, Pallas kernels for 0%

commit v1 on v0

--- a/solution.py
+++ b/solution.py
@@ -1,12 +1,377 @@
+import functools
+
 import jax
 import jax.numpy as jnp
 from jax import lax
+from jax.experimental import pallas as pl
+from jax.experimental.pallas import tpu as pltpu
 from jax.sharding import PartitionSpec as P
 
 GROUPS = 8
-
-
-def per_device(
+AXES = ("node", "local")
+F32 = jnp.float32
+BF16 = jnp.bfloat16
+
+Z_COUNT = 4
+
+
+def permutation(move):
+    pairs = []
+    for z in range(Z_COUNT):
+        for y in range(2):
+            for x in range(2):
+                for core in range(2):
+                    to_z, to_y, to_x, to_core = move(z, y, x, core)
+                    pairs.append(
+                        (
+                            ((z * 2 + y) * 2 + x) * 2 + core,
+                            (((to_z % Z_COUNT) * 2 + to_y) * 2 + to_x) * 2 + to_core,
+                        )
+                    )
+    return pairs
+
+
+CORE = permutation(lambda z, y, x, core: (z, y, x, 1 - core))
+ALONG_X = permutation(lambda z, y, x, core: (z, y, 1 - x, core))
+ALONG_Y = permutation(lambda z, y, x, core: (z, 1 - y, x, core))
+Z_UP = permutation(lambda z, y, x, core: (z + 1, y, x, core))
+Z_DOWN = permutation(lambda z, y, x, core: (z - 1, y, x, core))
+
+
+def send(value, pairs):
+    return lax.ppermute(value, AXES, pairs)
+
+
+def join(*values, axis=1):
+    return jnp.concatenate(values, axis=axis)
+
+
+def barrier(*values):
+    return lax.optimization_barrier(values)
+
+
+def expert_kernel(
+    source_count,
+    shared_count,
+    capacity,
+    weight_ref,
+    own_ref,
+    other_ref,
+    gate_ref,
+    up_ref,
+    down_ref,
+    *rest,
+):
+    if shared_count:
+        sgate_ref, sup_ref, sdown_ref = rest[:3]
+        rest = rest[3:]
+    own_out, other_out, rows, hidden, answers = rest[:5]
+    tokens = own_ref.shape[2]
+    width = own_ref.shape[3]
+    inner = gate_ref.shape[2]
+    weights = weight_ref[...]
+    hits = (weights > 0.0).astype(BF16)
+    earlier = (
+        lax.broadcasted_iota(jnp.int32, (tokens, tokens), 0)
+        < lax.broadcasted_iota(jnp.int32, (tokens, tokens), 1)
+    ).astype(BF16)
+    place = jnp.dot(hits, earlier, preferred_element_type=F32).astype(jnp.int32)
+    slots = lax.broadcasted_iota(jnp.int32, (capacity, tokens), 0)
+    source_of = []
+    for index in range(source_count):
+        chunk, core, block = index // 8, index // 4 % 2, index % 4
+        source_of.append((own_ref, own_out) if core == 0 else (other_ref, other_out))
+        chosen = (place[index : index + 1] == slots) & (weights[index : index + 1] > 0.0)
+        block_tokens = source_of[index][0][chunk, block]
+        rows[pl.ds(index * capacity, capacity)] = jnp.dot(
+            chosen.astype(BF16), block_tokens, preferred_element_type=F32
+        ).astype(BF16)
+
+    tile = 256
+    group = 8 * capacity
+
+    def up_step(step, carry):
+        columns = pl.ds(pl.multiple_of(step * tile, tile), tile)
+        for start in range(0, source_count * capacity, group):
+            block_rows = rows[pl.ds(start, group)]
+            gate_part = jnp.dot(block_rows, gate_ref[0, :, columns], preferred_element_type=F32)
+            up_part = jnp.dot(block_rows, up_ref[0, :, columns], preferred_element_type=F32)
+            hidden[pl.ds(start, group), columns] = (
+                gate_part / (1.0 + jnp.exp(-gate_part)) * up_part
+            ).astype(BF16)
+        return carry
+
+    lax.fori_loop(0, inner // tile, up_step, 0)
+
+    shared_hidden = None
+    if shared_count:
+        shared_rows = jnp.concatenate(
+            [own_ref[0, 0], own_ref[0, 1], other_ref[0, 0], other_ref[0, 1]], axis=0
+        )
+        gate_part = jnp.dot(shared_rows, sgate_ref[...], preferred_element_type=F32)
+        up_part = jnp.dot(shared_rows, sup_ref[...], preferred_element_type=F32)
+        rest[5][...] = (gate_part / (1.0 + jnp.exp(-gate_part)) * up_part).astype(BF16)
+
+    out_tile = 512
+
+    def down_step(step, carry):
+        columns = pl.ds(pl.multiple_of(step * out_tile, out_tile), out_tile)
+        for start in range(0, source_count * capacity, group):
+            answers[pl.ds(start, group)] = jnp.dot(
+                hidden[pl.ds(start, group)],
+                down_ref[0, :, columns],
+                preferred_element_type=F32,
+            ).astype(BF16)
+        for index in range(source_count):
+            chunk, core, block = index // 8, index // 4 % 2, index % 4
+            weight_row = weights[index : index + 1]
+            chosen = (place[index : index + 1] == slots) & (weight_row > 0.0)
+            spread = jnp.where(chosen, jnp.broadcast_to(weight_row, chosen.shape), 0.0)
+            high = spread.astype(BF16)
+            low = (spread - high.astype(F32)).astype(BF16)
+            answer = answers[pl.ds(index * capacity, capacity)]
+            total = lax.dot_general(
+                jnp.concatenate([high, low], axis=0),
+                jnp.concatenate([answer, answer], axis=0),
+                (((0,), (0,)), ((), ())),
+                preferred_element_type=F32,
+            )
+            if shared_count and chunk == 0 and block < 2:
+                total = total + jnp.dot(
+                    rest[5][pl.ds((core * 2 + block) * tokens, tokens)],
+                    sdown_ref[:, columns],
+                    preferred_element_type=F32,
+                )
+            source_of[index][1][chunk, block, :, columns] = total.astype(BF16)
+        return carry
+
+    lax.fori_loop(0, width // out_tile, down_step, 0)
+
+
+def expert_chunk(weights, own, other, expert_weights, shared_weights, capacity):
+    chunks, _, tokens, width = own.shape
+    source_count = chunks * 8
+    inner = expert_weights[0].shape[2]
+    shared_width = shared_weights[0].shape[1] if shared_weights else 0
+    scratch = [
+        pltpu.VMEM((source_count * capacity, width), BF16),
+        pltpu.VMEM((source_count * capacity, inner), BF16),
+        pltpu.VMEM((source_count * capacity, 512), BF16),
+    ]
+    if shared_weights:
+        scratch.append(pltpu.VMEM((4 * tokens, shared_width), BF16))
+    flops = 2 * source_count * capacity * (3 * width * inner + 2 * tokens * width)
+    operands = (weights, own, other, *expert_weights, *shared_weights)
+    return pl.pallas_call(
+        functools.partial(expert_kernel, source_count, len(shared_weights), capacity),
+        out_shape=[jax.ShapeDtypeStruct(own.shape, BF16)] * 2,
+        in_specs=[pl.BlockSpec(memory_space=pltpu.VMEM)] * len(operands),
+        out_specs=[pl.BlockSpec(memory_space=pltpu.VMEM)] * 2,
+        scratch_shapes=scratch,
+        cost_estimate=pl.CostEstimate(
+            flops=flops, bytes_accessed=3 * width * inner * 2 + 8 * own.size, transcendentals=0
+        ),
+        compiler_params=pltpu.CompilerParams(vmem_limit_bytes=56 * 1024 * 1024),
+    )(*operands)
+
+
+def route_table(group_choice, members, route_weight, expert_home, capacity):
+    tok_rows = members.shape[0]
+    experts_all = expert_home.shape[0]
+    per_group = experts_all // GROUPS
+    chosen = jnp.repeat(group_choice, 2, axis=1) * per_group + members
+    ids = jnp.arange(experts_all, dtype=jnp.int32)
+    target = jnp.sum(
+        jnp.where(chosen[:, :, None] == ids[None, None, :], expert_home[None, None, :], 0), axis=-1
+    )
+    table = jnp.sum(
+        jnp.where(target[:, :, None] == ids[None, None, :], route_weight[:, :, None], 0.0), axis=1
+    )
+    hits = (table > 0.0).astype(BF16)
+    earlier = (
+        lax.broadcasted_iota(jnp.int32, (tok_rows, tok_rows), 0)
+        > lax.broadcasted_iota(jnp.int32, (tok_rows, tok_rows), 1)
+    ).astype(BF16)
+    place = jnp.dot(earlier, hits, preferred_element_type=F32)
+    table = jnp.where(place < capacity, table, 0.0)
+    return table.T
+
+
+def block_device(
+    tokens,
+    group_choice,
+    members,
+    route_weight,
+    expert_home,
+    expert_gate,
+    expert_up,
+    expert_down,
+    shared_gate,
+    shared_up,
+    shared_down,
+):
+    tok_rows, width = tokens.shape
+    experts_all = expert_home.shape[0]
+    capacity = 2 * tok_rows * members.shape[1] // experts_all
+    expert_weights = (expert_gate, expert_up, expert_down)
+    shared_weights = (shared_gate, shared_up, shared_down)
+
+    rows_c, rows_b = tok_rows // 2, tok_rows * 3 // 8
+    c = tokens[None, :rows_c]
+    b = tokens[None, rows_c : rows_c + rows_b]
+    a = tokens[None, rows_c + rows_b :]
+    table = route_table(group_choice, members, route_weight, expert_home, capacity)
+
+    c1, c3, cx0, ax, by = (
+        send(c, Z_UP),
+        send(c, Z_DOWN),
+        send(c, ALONG_X),
+        send(a, ALONG_X),
+        send(b, ALONG_Y),
+    )
+    received = lax.all_to_all(table, AXES, split_axis=0, concat_axis=0, tiled=True)
+    c, b, a, c1, c3, cx0, ax, by = barrier(c, b, a, c1, c3, cx0, ax, by)
+    c0, b0, a0 = join(c, cx0, axis=0), join(b, by, axis=0), join(a, ax, axis=0)
+    c13 = jnp.stack([c1, c3])[:, 0]
+
+    c2, b1, b3, cx13, bx0, cy0, ay = (
+        send(c1, Z_UP),
+        send(b0, Z_UP),
+        send(b0, Z_DOWN),
+        send(c13, ALONG_X),
+        send(b0, ALONG_X),
+        send(c0, ALONG_Y),
+        send(a0, ALONG_Y),
+    )
+    c0, b0, a0, c13, c2, b1, b3, cx13, bx0, cy0, ay = barrier(
+        c0, b0, a0, c13, c2, b1, b3, cx13, bx0, cy0, ay
+    )
+    a0 = join(a0, ay, axis=0)
+    b13 = jnp.stack([b1, b3])
+    c13 = jnp.stack([c13, cx13], axis=1)
+    whole0 = jnp.stack(
+        [
+            jnp.concatenate([c0[0], b0[0], a0[0]]),
+            jnp.concatenate([c0[1], bx0[0], a0[1]]),
+            jnp.concatenate([cy0[0], b0[1], a0[2]]),
+            jnp.concatenate([cy0[1], bx0[1], a0[3]]),
+        ]
+    )[None]
+
+    b2, a1, a3, cx2, bx13, cy13, other0 = (
+        send(b1, Z_UP),
+        send(a0, Z_UP),
+        send(a0, Z_DOWN),
+        send(c2, ALONG_X),
+        send(b13, ALONG_X),
+        send(c13, ALONG_Y),
+        send(whole0, CORE),
+    )
+    b13, c13, c2, whole0, b2, a1, a3, cx2, bx13, cy13, other0 = barrier(
+        b13, c13, c2, whole0, b2, a1, a3, cx2, bx13, cy13, other0
+    )
+    c2 = join(c2, cx2, axis=0)
+    a13 = jnp.stack([a1, a3])
+    whole13 = jnp.stack(
+        [
+            jnp.concatenate([c13[:, 0], b13[:, 0], a13[:, 0]], axis=1),
+            jnp.concatenate([c13[:, 1], bx13[:, 0], a13[:, 1]], axis=1),
+            jnp.concatenate([cy13[:, 0], b13[:, 1], a13[:, 2]], axis=1),
+            jnp.concatenate([cy13[:, 1], bx13[:, 1], a13[:, 3]], axis=1),
+        ],
+        axis=1,
+    )
+
+    a2, bx2, cy2, other13 = (
+        send(a1, Z_UP),
+        send(b2, ALONG_X),
+        send(c2, ALONG_Y),
+        send(whole13, CORE),
+    )
+    whole2 = jnp.stack(
+        [
+            jnp.concatenate([c2[0], b2[0], a2[0]]),
+            jnp.concatenate([c2[1], bx2[0], a2[1]]),
+            jnp.concatenate([cy2[0], b2[1], a2[2]]),
+            jnp.concatenate([cy2[1], bx2[1], a2[3]]),
+        ]
+    )[None]
+    other2 = send(whole2, CORE)
+
+    node, local = lax.axis_index("node"), lax.axis_index("local")
+    z, y, x, core = node // 2, node % 2, local // 2, local % 2
+    order = []
+    for far_z in range(Z_COUNT):
+        for far_core in range(2):
+            for far_y in range(2):
+                for far_x in range(2):
+                    source = ((z - far_z) % Z_COUNT * 2 + (y ^ far_y)) * 2 + (x ^ far_x)
+                    order.append(source * 2 + (core ^ far_core))
+    weights = jnp.take(received, jnp.stack(order), axis=0)
+    weights13 = join(weights[8:16], weights[24:32], axis=0)
+
+    own0, far0 = expert_chunk(weights[:8], whole0, other0, expert_weights, shared_weights, capacity)
+    own13, far13 = expert_chunk(weights13, whole13, other13, expert_weights, (), capacity)
+    own2, far2 = expert_chunk(weights[16:24], whole2, other2, expert_weights, (), capacity)
+
+    def split(own, far):
+        total = own.astype(F32) + send(far, CORE).astype(F32)
+        part_c = total[:, :, :rows_c]
+        part_b = total[:, :, rows_c : rows_c + rows_b]
+        part_a = total[:, :, rows_c + rows_b :]
+        return part_c, part_b, part_a
+
+    def back(value, pairs):
+        return send(value.astype(BF16), pairs).astype(F32)
+
+    c2, b2, a2 = split(own2, far2)
+    sa2 = back(a2[0], Z_DOWN)
+    sb2 = back(b2[0, 1::2], ALONG_X)
+    sc2 = back(c2[0, 2:], ALONG_Y)
+    c13, b13, a13 = split(own13, far13)
+    c2, b2 = c2[0, :2], b2[0, 0::2]
+    c2, b2, c13, b13, a13, sa2, sb2, sc2 = barrier(c2, b2, c13, b13, a13, sa2, sb2, sc2)
+    c2, b2 = c2 + sc2, b2 + sb2
+    a1, a3 = a13[0] + sa2, a13[1]
+    sb = back(b2, Z_DOWN)
+    sa1 = back(a1, Z_DOWN)
+    sa3 = back(a3, Z_UP)
+    sc2 = back(c2[1], ALONG_X)
+    sb13 = back(b13[:, 1::2], ALONG_X)
+    sc13 = back(c13[:, 2:], ALONG_Y)
+    c0, b0, a0 = split(own0, far0)
+    c2, b13, c13 = c2[0], b13[:, 0::2], c13[:, :2]
+    c2, b13, c13, c0, b0, a0, sb, sa1, sa3, sc2, sb13, sc13 = barrier(
+        c2, b13, c13, c0, b0, a0, sb, sa1, sa3, sc2, sb13, sc13
+    )
+    c2 = c2 + sc2
+    b1, b3 = b13[0] + sb13[0] + sb, b13[1] + sb13[1]
+    c13 = c13 + sc13
+    a0 = a0[0] + sa1 + sa3
+    sc = back(c2, Z_DOWN)
+    sb1 = back(b1, Z_DOWN)
+    sb3 = back(b3, Z_UP)
+    sc13 = back(c13[:, 1], ALONG_X)
+    sb0 = back(b0[0, 1::2], ALONG_X)
+    sc0 = back(c0[0, 2:], ALONG_Y)
+    sa0 = back(a0[2:], ALONG_Y)
+    c13, b0, c0, a0 = c13[:, 0], b0[0, 0::2], c0[0, :2], a0[:2]
+    c13, b0, c0, a0, sc, sb1, sb3, sc13, sb0, sc0, sa0 = barrier(
+        c13, b0, c0, a0, sc, sb1, sb3, sc13, sb0, sc0, sa0
+    )
+    c1, c3 = c13[0] + sc13[0] + sc, c13[1] + sc13[1]
+    b0 = b0 + sb0 + sb1 + sb3
+    c0 = c0 + sc0
+    a0 = a0 + sa0
+    sc1 = back(c1, Z_DOWN)
+    sc3 = back(c3, Z_UP)
+    sc0 = back(c0[1], ALONG_X)
+    sa0 = back(a0[1], ALONG_X)
+    sb0 = back(b0[1], ALONG_Y)
+    return jnp.concatenate([c0[0] + sc0 + sc1 + sc3, b0[0] + sb0, a0[0] + sa0]).astype(BF16)
+
+
+def exchange_device(
     tokens,
     group_choice,
     members,
@@ -97,6 +462,11 @@
         P("local", None),
     )
     out_specs = P(("node", "local"), None)
+    whole_gather = mesh.shape["node"] == 2 * Z_COUNT and mesh.shape["local"] == 4
     return jax.shard_map(
-        per_device, mesh=mesh, in_specs=in_specs, out_specs=out_specs, check_vma=False
-    )
+        block_device if whole_gather else exchange_device,
+        mesh=mesh,
+        in_specs=in_specs,
+        out_specs=out_specs,
+        check_vma=False,
+    )

time: 512 us -> 271 us (0.53)
  blocking collectives: 191 us -> 0 us
  waiting for transfers between devices: 178 us -> 119 us
  Pallas kernels: 0 us -> 56.6 us
  starting transfers between devices: 4.25 us -> 52.8 us
  local copies, waits for them, and re-layouts: 65.6 us -> 24.9 us
  matrix products: 38.9 us -> 0.78 us
  between operations: 13.6 us -> 1.16 us
    all_to_all x1 -> x0, blocking collectives: 191 us -> none  [per_device(): lax.all_to_all(outgoing, ('node', 'local'), split_axis=0, concat_axis=0,...]
    ppermute x0 -> x48, waiting for transfers between devices: none -> 112 us  [send(): return lax.ppermute(value, AXES, pairs)]
    all_to_all x1, waiting for transfers between devices: 108 us -> 6.46 us  [block_device(): lax.all_to_all(table, AXES, split_axis=0, concat_axis=0, tiled=True)]
    all_gather x1 -> x0, waiting for transfers between devices: 69 us -> none  [per_device(): node_rows = lax.all_gather(tokens, 'local', axis=0, tiled=True)]
    pallas_call x0 -> x3, Pallas kernels: none -> 56.6 us  [expert_chunk(): pl.pallas_call(functools.partial(expert_kernel, source_count, len(shared_...]
    ppermute x0 -> x48, starting transfers between devices: none -> 48.7 us  [send(): return lax.ppermute(value, AXES, pairs)]
    dot_general x4 -> x1, matrix products: 38.9 us -> 0.78 us  [route_table(): place = jnp.dot(earlier, hits, preferred_element_type=F32)]
    gather x2 -> x1, local copies, waits for them, and re-layouts: 30.7 us -> 0.57 us  [block_device(): weights = jnp.take(received, jnp.stack(order), axis=0)]
  transfers between devices with their start and end apart: 3 -> 49, of which waited for: 2 -> 25; matrix products, arithmetic and copies ran while one was open for 9% -> 9% of each run, Pallas kernels for 0% -> 21%
where the time goes in v1:
time: 271 us
  waiting for transfers between devices  119 us (44%)
  Pallas kernels  56.6 us (21%)
  starting transfers between devices  52.8 us (19%)
  local copies, waits for them, and re-layouts  24.9 us (9%)
  other arithmetic  15.9 us (6%)
    ppermute x48, waiting for transfers between devices, send(): return lax.ppermute(value, AXES, pairs)  112 us
    pallas_call x3, Pallas kernels, expert_chunk(): pl.pallas_call(functools.partial(expert_kernel, source_count, len(shared_...  56.6 us
    ppermute x48, starting transfers between devices, send(): return lax.ppermute(value, AXES, pairs)  48.7 us
    unnamed x30, local copies, waits for them, and re-layouts  6.49 us
    all_to_all x1, waiting for transfers between devices, block_device(): lax.all_to_all(table, AXES, split_axis=0, concat_axis=0, tiled=True)  6.46 us
    add x2, other arithmetic, split(): total = own.astype(F32) + send(far, CORE).astype(F32)  6.3 us
  transfers between devices with their start and end apart: 49, of which 25 were waited for; matrix products, arithmetic and copies ran while one was open for 9% of the time, Pallas kernels for 21%

profile of v1, /device:TPU:0, one launch (start us, length us, event | category | flops | bytes accessed | tf_op | source)
XLA Modules:
  0.0 270.9 jit_solution(6249359525325132013)
XLA Ops:
  11.7 3.7 %collective-permute-done.3 = bf16[1,16,2048]{2,1,0:T(8,128)(2,1)S(1)} collective-permute-done((bf16[1,16,2048]{2,1,0:T(8,128)(2,1)S(1)}, bf16[1,16,2048]{2,1,0:T(8,128)(2,1)S(1)}, u32[]{:S(2)}, u32[]{:S(2)}) %collective-permute-start.3) | collective-permute-done | bytes 65568 | tf_op jit(solution)/shard_map/ppermute | solution.py:42
  23.3 3.5 %collective-permute-done.11 = bf16[2,16,2048]{2,1,0:T(8,128)(2,1)S(1)} collective-permute-done((bf16[2,16,2048]{2,1,0:T(8,128)(2,1)S(1)}, bf16[2,16,2048]{2,1,0:T(8,128)(2,1)S(1)}, u32[]{:S(2)}, u32[]{:S(2)}) %collective-permute-start.11) | collective-permute-done | bytes 131104 | tf_op jit(solution)/shard_map/ppermute | solution.py:42
  30.2 6.2 %collective-permute-done.6 = bf16[2,48,2048]{2,1,0:T(8,128)(2,1)S(1)} collective-permute-done((bf16[2,48,2048]{2,1,0:T(8,128)(2,1)S(1)}, bf16[2,48,2048]{2,1,0:T(8,128)(2,1)S(1)}, u32[]{:S(2)}, u32[]{:S(2)}) %collective-permute-start.6) | collective-permute-done | bytes 393248 | tf_op jit(solution)/shard_map/ppermute | solution.py:42
  36.4 7.4 %collective-permute-done.7 = bf16[2,48,2048]{2,1,0:T(8,128)(2,1)S(1)} collective-permute-done((bf16[2,48,2048]{2,1,0:T(8,128)(2,1)S(1)}, bf16[2,48,2048]{2,1,0:T(8,128)(2,1)S(1)}, u32[]{:S(2)}, u32[]{:S(2)}) %collective-permute-start.7) | collective-permute-done | bytes 393248 | tf_op jit(solution)/shard_map/ppermute | solution.py:42
  51.8 7.2 %collective-permute-done.13 = bf16[4,16,2048]{2,1,0:T(8,128)(2,1)S(1)} collective-permute-done((bf16[4,16,2048]{2,1,0:T(8,128)(2,1)S(1)}, bf16[4,16,2048]{2,1,0:T(8,128)(2,1)S(1)}, u32[]{:S(2)}, u32[]{:S(2)}) %collective-permute-start.13) | collective-permute-done | bytes 262176 | tf_op jit(solution)/shard_map/ppermute | solution.py:42
  62.5 9.1 %collective-permute-done.15 = bf16[1,64,2048]{2,1,0:T(8,128)(2,1)S(1)} collective-permute-done((bf16[1,64,2048]{2,1,0:T(8,128)(2,1)S(1)}, bf16[1,64,2048]{2,1,0:T(8,128)(2,1)S(1)}, u32[]{:S(2)}, u32[]{:S(2)}) %collective-permute-start.15) | collective-permute-done | bytes 262176 | tf_op jit(solution)/shard_map/ppermute | solution.py:42
  77.6 4.0 %collective-permute-done.19 = bf16[4,16,2048]{2,1,0:T(8,128)(2,1)S(1)} collective-permute-done((bf16[4,16,2048]{2,1,0:T(8,128)(2,1)S(1)}, bf16[4,16,2048]{2,1,0:T(8,128)(2,1)S(1)}, u32[]{:S(2)}, u32[]{:S(2)}) %collective-permute-start.19) | collective-permute-done | bytes 262176 | tf_op jit(solution)/shard_map/ppermute | solution.py:42
  81.6 5.3 %collective-permute-done.20 = bf16[2,48,2048]{2,1,0:T(8,128)(2,1)S(1)} collective-permute-done((bf16[2,48,2048]{2,1,0:T(8,128)(2,1)S(1)}, bf16[2,48,2048]{2,1,0:T(8,128)(2,1)S(1)}, u32[]{:S(2)}, u32[]{:S(2)}) %collective-permute-start.20) | collective-permute-done | bytes 393248 | tf_op jit(solution)/shard_map/ppermute | solution.py:42
  87.0 4.1 %collective-permute-done.21 = bf16[2,64,2048]{2,1,0:T(8,128)(2,1)S(1)} collective-permute-done((bf16[2,64,2048]{2,1,0:T(8,128)(2,1)S(1)}, bf16[2,64,2048]{2,1,0:T(8,128)(2,1)S(1)}, u32[]{:S(2)}, u32[]{:S(2)}) %collective-permute-start.21) | collective-permute-done | bytes 524320 | tf_op jit(solution)/shard_map/ppermute | solution.py:42
  92.8 4.1 %all-to-all-start = ((f32[32,1,128]{2,1,0:T(1,128)}), f32[32,1,128]{2,1,0:T(1,128)S(1)}, u32[]{:S(2)}, u32[]{:S(2)}) async-start(f32[32,1,128]{2,1,0:T(1,128)} %bitcast.35), calls=%async_computation | async-start | bytes 32768 | tf_op jit(solution)/shard_map/all_to_all | solution.py:232
  97.4 6.5 %all-to-all-done = f32[32,1,128]{2,1,0:T(1,128)S(1)} async-done(((f32[32,1,128]{2,1,0:T(1,128)}), f32[32,1,128]{2,1,0:T(1,128)S(1)}, u32[]{:S(2)}, u32[]{:S(2)}) %all-to-all-start) | async-done | bytes 16416 | tf_op jit(solution)/shard_map/all_to_all | solution.py:232
  105.1 17.5 %shard_map.111 = (bf16[1,4,128,2048]{3,2,1,0:T(8,128)(2,1)}, bf16[1,4,128,2048]{3,2,1,0:T(8,128)(2,1)}) custom-call(f32[8,128]{1,0:T(8,128)} %get-tuple-element.175.weight_ref, bf16[1,4,128,2048]{3,2,1,0:T(8,128)(2,1)} %copy-done.5, bf16[1,4,128,2048]{3,2,1,0:T(8,128)(2,1)} %collective-permute-done.18.other_ref, bf16[1,2048,768]{2,1,0:T(8,128)(2,1)} %gate_ref.5, ...), custom_call_target="tpu_custom_call" | custom-call | flops 5368709120 | bytes 17825792 | tf_op jit(solution)/shard_map/pallas_call | solution.py:165
  122.6 14.9 %shard_map.109 = (bf16[1,4,128,2048]{3,2,1,0:T(8,128)(2,1)}, bf16[1,4,128,2048]{3,2,1,0:T(8,128)(2,1)}) custom-call(f32[8,128]{1,0:T(8,128)} %get-tuple-element.178.weight_ref, bf16[1,4,128,2048]{3,2,1,0:T(8,128)(2,1)} %copy-done.6, bf16[1,4,128,2048]{3,2,1,0:T(8,128)(2,1)} %collective-permute-done.22.other_ref, bf16[1,2048,768]{2,1,0:T(8,128)(2,1)} %gate_ref.5, ...), custom_call_target="tpu_custom_call" | custom-call | flops 5368709120 | bytes 17825792 | tf_op jit(solution)/shard_map/pallas_call | solution.py:165
  138.6 4.9 %copy.24.own_ref = bf16[2,4,128,2048]{3,2,1,0:T(8,128)(2,1)} copy(bf16[2,4,128,2048]{3,2,0,1:T(8,128)(2,1)} %pad_maximum_fusion) | data formatting | bytes 8388608 | tf_op jit(solution)/shard_map/stack | solution.py:275
  143.5 4.8 %copy.25.other_ref = bf16[2,4,128,2048]{3,2,1,0:T(8,128)(2,1)} copy(bf16[2,4,128,2048]{3,2,0,1:T(8,128)(2,1)} %collective-permute-done.24) | data formatting | bytes 8388608 | tf_op jit(solution)/shard_map/ppermute | solution.py:42
  148.3 24.2 %shard_map.110 = (bf16[2,4,128,2048]{3,2,1,0:T(8,128)(2,1)}, bf16[2,4,128,2048]{3,2,1,0:T(8,128)(2,1)}) custom-call(f32[16,128]{1,0:T(8,128)} %pad_maximum_fusion.6.weight_ref, bf16[2,4,128,2048]{3,2,1,0:T(8,128)(2,1)} %copy.24.own_ref, bf16[2,4,128,2048]{3,2,1,0:T(8,128)(2,1)} %copy.25.other_ref, bf16[1,2048,768]{2,1,0:T(8,128)(2,1)} %gate_ref.5, ...), custom_call_target="tpu_custom_call" | custom-call | flops 10737418240 | bytes 26214400 | tf_op jit(solution)/shard_map/pallas_call | solution.py:165
  181.3 7.6 %collective-permute-done.26 = bf16[4,16,2048]{2,1,0:T(8,128)(2,1)S(1)} collective-permute-done((bf16[4,16,2048]{2,1,0:T(8,128)(2,1)S(1)}, bf16[4,16,2048]{2,1,0:T(8,128)(2,1)S(1)}, u32[]{:S(2)}, u32[]{:S(2)}) %collective-permute-start.26) | collective-permute-done | bytes 262176 | tf_op jit(solution)/shard_map/ppermute | solution.py:42
  195.6 4.0 %convert_add_fusion = f32[2,4,128,2048]{3,2,1,0:T(8,128)S(1)} fusion(bf16[2,4,128,2048]{3,2,1,0:T(8,128)(2,1)} %copy-done.3, bf16[2,4,128,2048]{3,2,1,0:T(8,128)(2,1)S(1)} %copy-done.2), kind=kLoop, calls=%fused_computation.1 | loop fusion | flops 6291456 | bytes 16777216 | tf_op jit(solution)/shard_map/add | solution.py:318
  207.8 4.0 %collective-permute-done.31 = bf16[4,16,2048]{2,1,0:T(8,128)(2,1)S(1)} collective-permute-done((bf16[4,16,2048]{2,1,0:T(8,128)(2,1)S(1)}, bf16[4,16,2048]{2,1,0:T(8,128)(2,1)S(1)}, u32[]{:S(2)}, u32[]{:S(2)}) %collective-permute-start.31) | collective-permute-done | bytes 262176 | tf_op jit(solution)/shard_map/ppermute | solution.py:42
  212.5 16.7 %collective-permute-done.33 = bf16[64,2048]{1,0:T(8,128)(2,1)S(1)} collective-permute-done((bf16[64,2048]{1,0:T(8,128)(2,1)S(1)}, bf16[64,2048]{1,0:T(8,128)(2,1)S(1)}, u32[]{:S(2)}, u32[]{:S(2)}) %collective-permute-start.33) | collective-permute-done | bytes 262176 | tf_op jit(solution)/shard_map/ppermute | solution.py:42
  238.9 3.7 %collective-permute-done.42 = bf16[2,16,2048]{2,1,0:T(8,128)(2,1)S(1)} collective-permute-done((bf16[2,16,2048]{2,1,0:T(8,128)(2,1)S(1)}, bf16[2,16,2048]{2,1,0:T(8,128)(2,1)S(1)}, u32[]{:S(2)}, u32[]{:S(2)}) %collective-permute-start.42) | collective-permute-done | bytes 131104 | tf_op jit(solution)/shard_map/ppermute | solution.py:42
  242.6 6.1 %collective-permute-done.36 = bf16[64,2048]{1,0:T(8,128)(2,1)S(1)} collective-permute-done((bf16[64,2048]{1,0:T(8,128)(2,1)S(1)}, bf16[64,2048]{1,0:T(8,128)(2,1)S(1)}, u32[]{:S(2)}, u32[]{:S(2)}) %collective-permute-start.36) | collective-permute-done | bytes 262176 | tf_op jit(solution)/shard_map/ppermute | solution.py:42
  249.5 6.1 %collective-permute-done.37 = bf16[2,48,2048]{2,1,0:T(8,128)(2,1)S(1)} collective-permute-done((bf16[2,48,2048]{2,1,0:T(8,128)(2,1)S(1)}, bf16[2,48,2048]{2,1,0:T(8,128)(2,1)S(1)}, u32[]{:S(2)}, u32[]{:S(2)}) %collective-permute-start.37) | collective-permute-done | bytes 393248 | tf_op jit(solution)/shard_map/ppermute | solution.py:42
  263.4 4.1 %collective-permute-done.47 = bf16[16,2048]{1,0:T(8,128)(2,1)S(1)} collective-permute-done((bf16[16,2048]{1,0:T(8,128)(2,1)S(1)}, bf16[16,2048]{1,0:T(8,128)(2,1)S(1)}, u32[]{:S(2)}, u32[]{:S(2)}) %collective-permute-start.47) | collective-permute-done | bytes 65568 | tf_op jit(solution)/shard_map/ppermute | solution.py:42
  (234 shorter events, 90.0 us)
Async XLA Ops:
  1.0 14.5 %collective-permute-start = (bf16[1,64,2048]{2,1,0:T(8,128)(2,1)S(1)}, bf16[1,64,2048]{2,1,0:T(8,128)(2,1)S(1)}, u32[]{:S(2)}, u32[]{:S(2)}) collective-permute-start(bf16[1,64,2048]{2,1,0:T(8,128)(2,1)S(1)} %slice_bitcast_fusion.26), channel_id=1, source_target_pairs={{0,8},{1,9},{2,10},{3,11},{4,12},{5,13},{6,14},{7,15},{8,16},{9,17... | collective-permute-start | bytes 786440 | tf_op jit(solution)/shard_map/ppermute | solution.py:42
  18.7 25.1 %collective-permute-start.8 = (bf16[2,64,2048]{2,1,0:T(8,128)(2,1)S(1)}, bf16[2,64,2048]{2,1,0:T(8,128)(2,1)S(1)}, u32[]{:S(2)}, u32[]{:S(2)}) collective-permute-start(bf16[2,64,2048]{2,1,0:T(8,128)(2,1)S(1)} %maximum_bitcast_fusion.6), channel_id=1, source_target_pairs={{0,2},{1,3},{2,0},{3,1},{4,6},{5,7},{6,4},{7,5},{8,10},{9,11},{10,... | collective-permute-start | bytes 1572872 | tf_op jit(solution)/shard_map/ppermute | solution.py:42
  21.9 21.9 %collective-permute-start.10 = (bf16[2,64,2048]{2,1,0:T(8,128)(2,1)S(1)}, bf16[2,64,2048]{2,1,0:T(8,128)(2,1)S(1)}, u32[]{:S(2)}, u32[]{:S(2)}) collective-permute-start(bf16[2,64,2048]{2,1,0:T(8,128)(2,1)S(1)} %constant_dynamic-update-slice_fusion), channel_id=1, source_target_pairs={{0,4},{1,5},{2,6},{3,7},{4,0},{5,1},{6,2},{7,3},{8,12},{9,13},{10,... | collective-permute-start | bytes 1572872 | tf_op jit(solution)/shard_map/ppermute | solution.py:42
  26.8 17.0 %collective-permute-start.7 = (bf16[2,48,2048]{2,1,0:T(8,128)(2,1)S(1)}, bf16[2,48,2048]{2,1,0:T(8,128)(2,1)S(1)}, u32[]{:S(2)}, u32[]{:S(2)}) collective-permute-start(bf16[2,48,2048]{2,1,0:T(8,128)(2,1)S(1)} %constant_dynamic-update-slice_fusion.2), channel_id=1, source_target_pairs={{0,24},{1,25},{2,26},{3,27},{4,28},{5,29},{6,30},{7,31},{8,0},{9,1... | collective-permute-start | bytes 1179656 | tf_op jit(solution)/shard_map/ppermute | solution.py:42
  29.5 14.3 %collective-permute-start.9 = (bf16[2,48,2048]{2,1,0:T(8,128)(2,1)S(1)}, bf16[2,48,2048]{2,1,0:T(8,128)(2,1)S(1)}, u32[]{:S(2)}, u32[]{:S(2)}) collective-permute-start(bf16[2,48,2048]{2,1,0:T(8,128)(2,1)S(1)} %constant_dynamic-update-slice_fusion.2), channel_id=1, source_target_pairs={{0,2},{1,3},{2,0},{3,1},{4,6},{5,7},{6,4},{7,5},{8,10},{9,11},{10,... | collective-permute-start | bytes 1179656 | tf_op jit(solution)/shard_map/ppermute | solution.py:42
  44.5 27.5 %collective-permute-start.18 = (bf16[1,4,128,2048]{3,2,1,0:T(8,128)(2,1)S(1)}, bf16[1,4,128,2048]{3,2,1,0:T(8,128)(2,1)}, u32[]{:S(2)}, u32[]{:S(2)}) collective-permute-start(bf16[1,4,128,2048]{3,2,1,0:T(8,128)(2,1)S(1)} %maximum_bitcast_fusion.own_ref), channel_id=1, source_target_pairs={{0,1},{1,0},{2,3},{3,2},{4,5},{5,4},{6,7},{7,6},{8,9},{9,8},{10,11... | collective-permute-start | bytes 6291464 | tf_op jit(solution)/shard_map/ppermute | solution.py:42
  44.7 27.4 %collective-permute-start.17 = (bf16[2,2,64,2048]{3,2,0,1:T(8,128)(2,1)S(1)}, bf16[2,2,64,2048]{3,2,0,1:T(8,128)(2,1)S(1)}, u32[]{:S(2)}, u32[]{:S(2)}) collective-permute-start(bf16[2,2,64,2048]{3,2,0,1:T(8,128)(2,1)S(1)} %pad_maximum_fusion.1), channel_id=1, source_target_pairs={{0,4},{1,5},{2,6},{3,7},{4,0},{5,1},{6,2},{7,3},{8,12},{9,13},{10,... | collective-permute-start | bytes 3145736 | tf_op jit(solution)/shard_map/ppermute | solution.py:42
  46.3 25.7 %collective-permute-start.16 = (bf16[2,2,48,2048]{3,2,1,0:T(8,128)(2,1)S(1)}, bf16[2,2,48,2048]{3,2,1,0:T(8,128)(2,1)S(1)}, u32[]{:S(2)}, u32[]{:S(2)}) collective-permute-start(bf16[2,2,48,2048]{3,2,1,0:T(8,128)(2,1)S(1)} %pad_maximum_fusion.2), channel_id=1, source_target_pairs={{0,2},{1,3},{2,0},{3,1},{4,6},{5,7},{6,4},{7,5},{8,10},{9,11},{10,... | collective-permute-start | bytes 2359304 | tf_op jit(solution)/shard_map/ppermute | solution.py:42
  75.4 68.1 %collective-permute-start.24 = (bf16[2,4,128,2048]{3,2,0,1:T(8,128)(2,1)}, bf16[2,4,128,2048]{3,2,0,1:T(8,128)(2,1)}, u32[]{:S(2)}, u32[]{:S(2)}) collective-permute-start(bf16[2,4,128,2048]{3,2,0,1:T(8,128)(2,1)} %pad_maximum_fusion), channel_id=1, source_target_pairs={{0,1},{1,0},{2,3},{3,2},{4,5},{5,4},{6,7},{7,6},{8,9},{9,8},{10,11... | collective-permute-start | bytes 12582920 | tf_op jit(solution)/shard_map/ppermute | solution.py:42
  77.0 14.1 %collective-permute-start.21 = (bf16[2,64,2048]{2,1,0:T(8,128)(2,1)S(1)}, bf16[2,64,2048]{2,1,0:T(8,128)(2,1)S(1)}, u32[]{:S(2)}, u32[]{:S(2)}) collective-permute-start(bf16[2,64,2048]{2,1,0:T(8,128)(2,1)S(1)} %pad_maximum_fusion.3), channel_id=1, source_target_pairs={{0,4},{1,5},{2,6},{3,7},{4,0},{5,1},{6,2},{7,3},{8,12},{9,13},{10,... | collective-permute-start | bytes 1572872 | tf_op jit(solution)/shard_map/ppermute | solution.py:42
  91.5 31.1 %collective-permute-start.22 = (bf16[1,4,128,2048]{3,2,1,0:T(8,128)(2,1)S(1)}, bf16[1,4,128,2048]{3,2,1,0:T(8,128)(2,1)}, u32[]{:S(2)}, u32[]{:S(2)}) collective-permute-start(bf16[1,4,128,2048]{3,2,1,0:T(8,128)(2,1)S(1)} %maximum_bitcast_fusion.1.own_ref), channel_id=1, source_target_pairs={{0,1},{1,0},{2,3},{3,2},{4,5},{5,4},{6,7},{7,6},{8,9},{9,8},{10,11... | collective-permute-start | bytes 6291464 | tf_op jit(solution)/shard_map/ppermute | solution.py:42
  122.6 50.0 %collective-permute-start.29 = (bf16[1,4,128,2048]{3,2,1,0:T(8,128)(2,1)}, bf16[1,4,128,2048]{3,2,1,0:T(8,128)(2,1)}, u32[]{:S(2)}, u32[]{:S(2)}) collective-permute-start(bf16[1,4,128,2048]{3,2,1,0:T(8,128)(2,1)} %get-tuple-element.111), channel_id=1, source_target_pairs={{0,1},{1,0},{2,3},{3,2},{4,5},{5,4},{6,7},{7,6},{8,9},{9,8},{10,11... | collective-permute-start | bytes 6291464 | tf_op jit(solution)/shard_map/ppermute | solution.py:42
  137.5 39.5 %collective-permute-start.23 = (bf16[1,4,128,2048]{3,2,1,0:T(8,128)(2,1)}, bf16[1,4,128,2048]{3,2,1,0:T(8,128)(2,1)S(1)}, u32[]{:S(2)}, u32[]{:S(2)}) collective-permute-start(bf16[1,4,128,2048]{3,2,1,0:T(8,128)(2,1)} %get-tuple-element.96), channel_id=1, source_target_pairs={{0,1},{1,0},{2,3},{3,2},{4,5},{5,4},{6,7},{7,6},{8,9},{9,8},{10,11... | collective-permute-start | bytes 6291464 | tf_op jit(solution)/shard_map/ppermute | solution.py:42
  172.5 21.1 %collective-permute-start.25 = (bf16[2,4,128,2048]{3,2,1,0:T(8,128)(2,1)}, bf16[2,4,128,2048]{3,2,1,0:T(8,128)(2,1)S(1)}, u32[]{:S(2)}, u32[]{:S(2)}) collective-permute-start(bf16[2,4,128,2048]{3,2,1,0:T(8,128)(2,1)} %get-tuple-element.103), channel_id=1, source_target_pairs={{0,1},{1,0},{2,3},{3,2},{4,5},{5,4},{6,7},{7,6},{8,9},{9,8},{10,11... | collective-permute-start | bytes 12582920 | tf_op jit(solution)/shard_map/ppermute | solution.py:42
  179.1 14.4 %collective-permute-start.28 = (bf16[2,64,2048]{2,1,0:T(8,128)(2,1)S(1)}, bf16[2,64,2048]{2,1,0:T(8,128)(2,1)S(1)}, u32[]{:S(2)}, u32[]{:S(2)}) collective-permute-start(bf16[2,64,2048]{2,1,0:T(8,128)(2,1)S(1)} %slice_bitcast_fusion.7), channel_id=1, source_target_pairs={{0,4},{1,5},{2,6},{3,7},{4,0},{5,1},{6,2},{7,3},{8,12},{9,13},{10,... | collective-permute-start | bytes 1572872 | tf_op jit(solution)/shard_map/ppermute | solution.py:42
  203.3 26.0 %collective-permute-start.30 = (bf16[2,48,2048]{2,1,0:T(8,128)(2,1)S(1)}, bf16[2,48,2048]{2,1,0:T(8,128)(2,1)S(1)}, u32[]{:S(2)}, u32[]{:S(2)}) collective-permute-start(bf16[2,48,2048]{2,1,0:T(8,128)(2,1)S(1)} %add_convert_fusion.1), channel_id=1, source_target_pairs={{0,24},{1,25},{2,26},{3,27},{4,28},{5,29},{6,30},{7,31},{8,0},{9,1... | collective-permute-start | bytes 1179656 | tf_op jit(solution)/shard_map/ppermute | solution.py:42
  204.9 24.5 %collective-permute-start.34 = (bf16[2,2,48,2048]{3,2,1,0:T(8,128)(2,1)S(1)}, bf16[2,2,48,2048]{3,2,1,0:T(8,128)(2,1)S(1)}, u32[]{:S(2)}, u32[]{:S(2)}) collective-permute-start(bf16[2,2,48,2048]{3,2,1,0:T(8,128)(2,1)S(1)} %slice.325), channel_id=1, source_target_pairs={{0,2},{1,3},{2,0},{3,1},{4,6},{5,7},{6,4},{7,5},{8,10},{9,11},{10,... | collective-permute-start | bytes 2359304 | tf_op jit(solution)/shard_map/ppermute | solution.py:42
  205.5 24.0 %collective-permute-start.35 = (bf16[2,2,64,2048]{3,2,1,0:T(8,128)(2,1)S(1)}, bf16[2,2,64,2048]{3,2,1,0:T(8,128)(2,1)S(1)}, u32[]{:S(2)}, u32[]{:S(2)}) collective-permute-start(bf16[2,2,64,2048]{3,2,1,0:T(8,128)(2,1)S(1)} %slice.521), channel_id=1, source_target_pairs={{0,4},{1,5},{2,6},{3,7},{4,0},{5,1},{6,2},{7,3},{8,12},{9,13},{10,... | collective-permute-start | bytes 3145736 | tf_op jit(solution)/shard_map/ppermute | solution.py:42
  206.2 22.9 %collective-permute-start.33 = (bf16[64,2048]{1,0:T(8,128)(2,1)S(1)}, bf16[64,2048]{1,0:T(8,128)(2,1)S(1)}, u32[]{:S(2)}, u32[]{:S(2)}) collective-permute-start(bf16[64,2048]{1,0:T(8,128)(2,1)S(1)} %fusion.16), channel_id=1, source_target_pairs={{0,2},{1,3},{2,0},{3,1},{4,6},{5,7},{6,4},{7,5},{8,10},{9,11},{10,... | collective-permute-start | bytes 786440 | tf_op jit(solution)/shard_map/ppermute | solution.py:42
  211.8 17.4 %collective-permute-start.32 = (bf16[4,16,2048]{2,1,0:T(8,128)(2,1)S(1)}, bf16[4,16,2048]{2,1,0:T(8,128)(2,1)S(1)}, u32[]{:S(2)}, u32[]{:S(2)}) collective-permute-start(bf16[4,16,2048]{2,1,0:T(8,128)(2,1)S(1)} %fusion.15), channel_id=1, source_target_pairs={{0,8},{1,9},{2,10},{3,11},{4,12},{5,13},{6,14},{7,15},{8,16},{9,17... | collective-permute-start | bytes 786440 | tf_op jit(solution)/shard_map/ppermute | solution.py:42
  231.9 17.6 %collective-permute-start.38 = (bf16[2,48,2048]{2,1,0:T(8,128)(2,1)S(1)}, bf16[2,48,2048]{2,1,0:T(8,128)(2,1)S(1)}, u32[]{:S(2)}, u32[]{:S(2)}) collective-permute-start(bf16[2,48,2048]{2,1,0:T(8,128)(2,1)S(1)} %fusion.11), channel_id=1, source_target_pairs={{0,8},{1,9},{2,10},{3,11},{4,12},{5,13},{6,14},{7,15},{8,16},{9,17... | collective-permute-start | bytes 1179656 | tf_op jit(solution)/shard_map/ppermute | solution.py:42
  232.6 16.2 %collective-permute-start.36 = (bf16[64,2048]{1,0:T(8,128)(2,1)S(1)}, bf16[64,2048]{1,0:T(8,128)(2,1)S(1)}, u32[]{:S(2)}, u32[]{:S(2)}) collective-permute-start(bf16[64,2048]{1,0:T(8,128)(2,1)S(1)} %add_convert_fusion.3), channel_id=1, source_target_pairs={{0,24},{1,25},{2,26},{3,27},{4,28},{5,29},{6,30},{7,31},{8,0},{9,1... | collective-permute-start | bytes 786440 | tf_op jit(solution)/shard_map/ppermute | solution.py:42
  236.7 20.2 %collective-permute-start.39 = (bf16[2,64,2048]{2,1,0:T(8,128)(2,1)S(1)}, bf16[2,64,2048]{2,1,0:T(8,128)(2,1)S(1)}, u32[]{:S(2)}, u32[]{:S(2)}) collective-permute-start(bf16[2,64,2048]{2,1,0:T(8,128)(2,1)S(1)} %fusion.2), channel_id=1, source_target_pairs={{0,2},{1,3},{2,0},{3,1},{4,6},{5,7},{6,4},{7,5},{8,10},{9,11},{10,... | collective-permute-start | bytes 1572872 | tf_op jit(solution)/shard_map/ppermute | solution.py:42
  237.4 19.6 %collective-permute-start.41 = (bf16[2,64,2048]{2,1,0:T(8,128)(2,1)S(1)}, bf16[2,64,2048]{2,1,0:T(8,128)(2,1)S(1)}, u32[]{:S(2)}, u32[]{:S(2)}) collective-permute-start(bf16[2,64,2048]{2,1,0:T(8,128)(2,1)S(1)} %fusion.3), channel_id=1, source_target_pairs={{0,4},{1,5},{2,6},{3,7},{4,0},{5,1},{6,2},{7,3},{8,12},{9,13},{10,... | collective-permute-start | bytes 1572872 | tf_op jit(solution)/shard_map/ppermute | solution.py:42
  (41 other events, 354.4 us)
